TPU v7x, 32 devices: a whole 2x2x4 slice. The times are simulated.
32 devices in a mesh: dp: 4 (over y, x), tm: 4 (over z), height: 2 (over core).
Axes of the slice: x: 2, y: 2, z: 4, core: 2. Of those that a mesh axis runs over, the one named last changes fastest.
Arguments:
- video: bfloat16 [4, 8, 8, 64, 256], P('dp', 'tm', 'height'), may hold values from -6 to 6
- lengths: int32 [4], P('dp'), may hold values from 1 to 8
- enc_weight: bfloat16 [3, 3, 3, 256, 256], replicated, may hold values from -0.078125 to 0.078125
- dec_weight: bfloat16 [3, 3, 3, 256, 256], replicated, may hold values from -0.078125 to 0.078125
- cotangent: bfloat16 [4, 8, 8, 64, 256], P('dp', 'tm', 'height'), may hold values from -6 to 6
Outputs:
- output: bfloat16 [4, 8, 8, 64, 256], P('dp', 'tm', 'height')
- enc_grad: float32 [3, 3, 3, 256, 256], replicated
- dec_grad: float32 [3, 3, 3, 256, 256], replicated
All inputs are finite; a program needn't handle non-finite values.
Results may differ from a plain program's by a relative error of at most 0.0045.
Values may be sent and summed in bfloat16 or wider, within the bound.
A program may use at most 128 MiB of HBM per device.

v0:
```python
import jax
import jax.numpy as jnp
from jax import lax
from jax.sharding import PartitionSpec as P


def extended(shard, sides, width):
    for axis, dim in sides:
        devices, length = (lax.axis_size(axis), shard.shape[dim])
        up = [(i, (i + 1) % devices) for i in range(devices - 1)]
        down = [(j, i) for i, j in up]
        last = lax.slice_in_dim(shard, length - width, length, axis=dim)
        leading = lax.slice_in_dim(shard, 0, width, axis=dim)
        before = lax.ppermute(last, axis, up)
        after = lax.ppermute(leading, axis, down)
        shard = jnp.concatenate([before, shard, after], axis=dim)
    return shard


def from_behind(block, axis, distance):
    devices = range(lax.axis_size(axis))
    route = [(i - distance, i) for i in devices if i - distance in devices]
    return lax.ppermute(block, axis, route)


def apply_taps(ext, weight):
    count, frame_pad, row_pad, wide, chans = ext.shape
    frames = frame_pad - 2
    rows = row_pad - 2
    outs = weight.shape[-1]
    padded = jnp.pad(ext, ((0, 0), (0, 0), (0, 0), (1, 1), (0, 0)))
    stacked = jnp.concatenate([padded[:, :, :, e : e + wide, :] for e in range(3)], axis=-1)
    total = jnp.zeros((count * frames * rows * wide, outs), jnp.float32)
    for a in range(3):
        for b in range(3):
            slab = stacked[:, a : a + frames, b : b + rows].reshape(-1, 3 * chans)
            total = total + jnp.dot(
                slab, weight[a, b].reshape(3 * chans, outs), preferred_element_type=jnp.float32
            )
    return total.reshape(count, frames, rows, wide, outs)


def tap_grads(ext, cot):
    count, frame_pad, row_pad, wide, chans = ext.shape
    frames = frame_pad - 2
    rows = row_pad - 2
    outs = cot.shape[-1]
    padded = jnp.pad(ext, ((0, 0), (0, 0), (0, 0), (1, 1), (0, 0)))
    stacked = jnp.concatenate([padded[:, :, :, e : e + wide, :] for e in range(3)], axis=-1)
    flat = cot.reshape(-1, outs)
    result = []
    for a in range(3):
        for b in range(3):
            slab = stacked[:, a : a + frames, b : b + rows].reshape(-1, 3 * chans)
            result.append(
                lax.dot_general(
                    slab, flat, (((0,), (0,)), ((), ())), preferred_element_type=jnp.float32
                )
            )
    return jnp.stack(result).reshape(3, 3, 3, chans, outs)


def dsilu(value):
    sig = jax.nn.sigmoid(value)
    return sig * (1.0 + value * (1.0 - sig))


def row_edges(block):
    return extended(block, (("height", 2),), 1)


def with_earlier(block):
    before = from_behind(block, "tm", 1)
    return row_edges(jnp.concatenate([before, block], axis=1))


def with_later(block):
    after = from_behind(block, "tm", -1)
    return row_edges(jnp.concatenate([block, after], axis=1))


def shards(video, lengths, enc_weight, dec_weight, cotangent):
    frames = video.shape[1]
    first_frame = lax.axis_index("tm") * frames
    tpos = first_frame + jnp.arange(frames, dtype=jnp.int32)
    keep = (tpos[None, :] < lengths[:, None])[:, :, None, None, None]
    masked = jnp.where(keep, video, jnp.zeros_like(video))
    cot_masked = jnp.where(keep, cotangent, jnp.zeros_like(cotangent))
    ext_x = with_earlier(masked)
    pre = apply_taps(ext_x, enc_weight)
    hidden = jax.nn.silu(pre).astype(jnp.bfloat16)
    ext_h = with_earlier(hidden)
    output = (apply_taps(ext_h, dec_weight) + masked.astype(jnp.float32)).astype(jnp.bfloat16)
    ext_g = with_later(cot_masked)
    flipped = jnp.transpose(dec_weight[::-1, ::-1, ::-1], (0, 1, 2, 4, 3))
    dec_local = tap_grads(ext_h, cot_masked)
    back = apply_taps(ext_g, flipped)
    dpre = (back * dsilu(pre)).astype(jnp.bfloat16)
    enc_local = tap_grads(ext_x, dpre)
    enc_grad, dec_grad = lax.psum((enc_local, dec_local), ("dp", "tm", "height"))
    return (output, enc_grad, dec_grad)


def solution(mesh):
    in_specs = (
        P("dp", "tm", "height", None, None),
        P("dp"),
        P(),
        P(),
        P("dp", "tm", "height", None, None),
    )
    out_specs = (P("dp", "tm", "height", None, None), P(), P())
    return jax.shard_map(shards, mesh=mesh, in_specs=in_specs, out_specs=out_specs, check_vma=False)
```

profile of v0, /device:TPU:0, one launch (start us, length us, event | category | flops | bytes accessed | tf_op | source)
XLA Modules:
  0.0 335.8 jit_solution(2890737925385777214)
XLA Ops:
  7.9 1.1 broadcast_select_fusion
  9.0 4.9 %collective-permute-start = (bf16[1,2,4,64,256]{4,3,2,1,0:T(8,128)(2,1)S(1)}, bf16[1,2,4,64,256]{4,3,2,1,0:T(8,128)(2,1)S(1)}, u32[]{:S(2)}, u32[]{:S(2)}) collective-permute-start(bf16[1,2,4,64,256]{4,3,2,1,0:T(8,128)(2,1)S(1)} %get-tuple-element.72), channel_id=1, source_target_pairs={{0,2},{2,4},{4,6},{1,3},{3,5},{5,7},{8,10},{10,12},{12,14},{9,11},... | collective-permute-start | bytes 786440 | tf_op jit(solution)/shard_map/ppermute | solution.py:23
  14.0 1.3 collective-permute-start.6
  15.3 6.0 %copy.8 = bf16[3,3,3,256,256]{3,4,2,1,0:T(8,128)(2,1)} copy(bf16[3,3,3,256,256]{4,3,2,1,0:T(8,128)(2,1)} %param.8) | data formatting | bytes 7077888 | tf_op args[3]
  21.3 2.4 reverse_bitcast_fusion
  24.1 1.6 collective-permute-start.7
  25.7 1.3 collective-permute-start.8
  27.4 3.0 collective-permute-start.1
  30.4 1.3 collective-permute-start.2
  31.8 0.5 select_maximum_fusion
  32.3 0.5 fusion.103
  32.8 0.9 collective-permute-done.2
  33.7 0.5 fusion.49
  34.2 0.5 fusion.105
  35.0 0.9 fusion.100
  36.2 0.9 fusion.102
  37.0 0.4 fusion.113
  38.6 0.4 fusion.109
  38.9 0.4 fusion.108
  39.7 0.4 fusion.106
  40.1 0.5 fusion.40
  40.7 4.6 %collective-permute-start.3 = (bf16[1,2,4,64,256]{4,3,2,1,0:T(8,128)(2,1)S(1)}, bf16[1,2,4,64,256]{4,3,2,1,0:T(8,128)(2,1)S(1)}, u32[]{:S(2)}, u32[]{:S(2)}) collective-permute-start(bf16[1,2,4,64,256]{4,3,2,1,0:T(8,128)(2,1)S(1)} %multiply_convert_fusion), channel_id=1, source_target_pairs={{0,2},{2,4},{4,6},{1,3},{3,5},{5,7},{8,10},{10,12},{12,14},{9,11},... | collective-permute-start | bytes 786440 | tf_op jit(solution)/shard_map/ppermute | solution.py:23
  45.7 0.4 fusion.128
  46.0 0.4 fusion.127
  46.8 0.4 fusion.125
  47.2 0.4 fusion.124
  47.9 0.4 fusion.122
  48.3 0.6 fusion.41
  48.9 0.4 fusion.18
  49.4 0.4 fusion.17
  49.8 0.4 fusion.16
  50.2 0.4 fusion.15
  50.6 0.4 fusion.14
  51.0 0.4 fusion.13
  51.5 0.4 fusion.12
  51.9 0.4 fusion.11
  52.4 1.8 collective-permute-start.4
  54.2 1.5 collective-permute-start.5
  55.7 0.4 fusion.10
  56.2 1.3 collective-permute-done.5
  57.4 0.5 select_maximum_fusion.3
  57.9 0.5 fusion.104
  58.7 0.4 copy-done.1
  59.1 1.3 fusion.9
  60.4 1.3 fusion.8
  61.7 1.3 fusion.7
  63.0 1.3 fusion.6
  64.3 1.3 fusion.5
  65.5 1.3 fusion.4
  66.8 1.3 fusion.3
  68.1 1.3 fusion.2
  69.4 1.3 fusion.1
  70.7 2.3 fusion.98
  73.1 0.9 fusion.101
  73.9 0.4 fusion.121
  74.3 0.4 fusion.120
  74.7 0.4 fusion.119
  75.4 0.4 fusion.117
  76.2 0.4 fusion.115
  77.0 0.4 fusion.35
  77.4 0.8 add_convert_fusion
  78.2 240.9 %all-reduce.6.cloned.1.call-done = (f32[3,3,3,256,256]{4,3,2,1,0:T(8,128)}, f32[3,3,3,256,256]{4,3,2,1,0:T(8,128)}) async-done(((f32[3,3,3,256,256]{4,3,2,1,0:T(8,128)}, f32[3,3,3,256,256]{4,3,2,1,0:T(8,128)}), (f32[3,3,3,256,256]{4,3,2,1,0:T(8,128)}, f32[3,3,3,256,256]{4,3,2,1,0:T(8,128)})) %all-reduce.6.cloned.1.call-update) | async-done | bytes 14155792 | tf_op jit(solution)/shard_map/psum | solution.py:100
  319.1 6.9 %copy.46 = f32[3,3,3,256,256]{4,3,2,1,0:T(8,128)} copy(f32[3,3,3,256,256]{4,3,2,1,0:T(8,128)} %get-tuple-element.74) | data formatting | bytes 14155776
  326.0 3.0 copy.47
  (34 shorter events, 5.6 us)
Async XLA Ops:
  7.2 311.9 %all-reduce.6.cloned.1.call-start = ((), (), s32[]{:S(2)}) async-start(), calls=%async_computation | async-start | bytes 28311552 | tf_op jit(solution)/shard_map/psum | solution.py:100
  9.0 18.3 %collective-permute-start = (bf16[1,2,4,64,256]{4,3,2,1,0:T(8,128)(2,1)S(1)}, bf16[1,2,4,64,256]{4,3,2,1,0:T(8,128)(2,1)S(1)}, u32[]{:S(2)}, u32[]{:S(2)}) collective-permute-start(bf16[1,2,4,64,256]{4,3,2,1,0:T(8,128)(2,1)S(1)} %get-tuple-element.72), channel_id=1, source_target_pairs={{0,2},{2,4},{4,6},{1,3},{3,5},{5,7},{8,10},{10,12},{12,14},{9,11},... | collective-permute-start | bytes 786440 | tf_op jit(solution)/shard_map/ppermute | solution.py:23
  14.0 10.1 %collective-permute-start.6 = (bf16[1,2,4,64,256]{4,3,2,1,0:T(8,128)(2,1)S(1)}, bf16[1,2,4,64,256]{4,3,2,1,0:T(8,128)(2,1)S(1)}, u32[]{:S(2)}, u32[]{:S(2)}) collective-permute-start(bf16[1,2,4,64,256]{4,3,2,1,0:T(8,128)(2,1)S(1)} %get-tuple-element.71), channel_id=1, source_target_pairs={{2,0},{4,2},{6,4},{3,1},{5,3},{7,5},{10,8},{12,10},{14,12},{11,9},... | collective-permute-start | bytes 786440 | tf_op jit(solution)/shard_map/ppermute | solution.py:23
  23.7 3.3 copy-start.2
  24.1 7.7 %collective-permute-start.7 = (bf16[1,4,1,64,256]{4,3,2,1,0:T(8,128)(2,1)S(1)}, bf16[1,4,1,64,256]{4,3,2,1,0:T(8,128)(2,1)S(1)}, u32[]{:S(2)}, u32[]{:S(2)}) collective-permute-start(bf16[1,4,1,64,256]{4,3,2,1,0:T(8,128)(2,1)S(1)} %get-tuple-element.65), channel_id=1, source_target_pairs={{0,1},{2,3},{4,5},{6,7},{8,9},{10,11},{12,13},{14,15},{16,17},{18,... | collective-permute-start | bytes 393224 | tf_op jit(solution)/shard_map/ppermute | solution.py:14
  25.7 6.1 %collective-permute-start.8 = (bf16[1,4,1,64,256]{4,3,2,1,0:T(8,128)(2,1)S(1)}, bf16[1,4,1,64,256]{4,3,2,1,0:T(8,128)(2,1)S(1)}, u32[]{:S(2)}, u32[]{:S(2)}) collective-permute-start(bf16[1,4,1,64,256]{4,3,2,1,0:T(8,128)(2,1)S(1)} %get-tuple-element.66), channel_id=1, source_target_pairs={{1,0},{3,2},{5,4},{7,6},{9,8},{11,10},{13,12},{15,14},{17,16},{19,... | collective-permute-start | bytes 393224 | tf_op jit(solution)/shard_map/ppermute | solution.py:15
  27.4 5.4 %collective-permute-start.1 = (bf16[1,4,1,64,256]{4,3,2,1,0:T(8,128)(2,1)S(1)}, bf16[1,4,1,64,256]{4,3,2,1,0:T(8,128)(2,1)S(1)}, u32[]{:S(2)}, u32[]{:S(2)}) collective-permute-start(bf16[1,4,1,64,256]{4,3,2,1,0:T(8,128)(2,1)S(1)} %get-tuple-element.69), channel_id=1, source_target_pairs={{0,1},{2,3},{4,5},{6,7},{8,9},{10,11},{12,13},{14,15},{16,17},{18,... | collective-permute-start | bytes 393224 | tf_op jit(solution)/shard_map/ppermute | solution.py:14
  30.4 3.2 collective-permute-start.2
  40.7 11.6 %collective-permute-start.3 = (bf16[1,2,4,64,256]{4,3,2,1,0:T(8,128)(2,1)S(1)}, bf16[1,2,4,64,256]{4,3,2,1,0:T(8,128)(2,1)S(1)}, u32[]{:S(2)}, u32[]{:S(2)}) collective-permute-start(bf16[1,2,4,64,256]{4,3,2,1,0:T(8,128)(2,1)S(1)} %multiply_convert_fusion), channel_id=1, source_target_pairs={{0,2},{2,4},{4,6},{1,3},{3,5},{5,7},{8,10},{10,12},{12,14},{9,11},... | collective-permute-start | bytes 786440 | tf_op jit(solution)/shard_map/ppermute | solution.py:23
  52.4 3.8 %collective-permute-start.4 = (bf16[1,4,1,64,256]{4,3,2,1,0:T(8,128)(2,1)S(1)}, bf16[1,4,1,64,256]{4,3,2,1,0:T(8,128)(2,1)S(1)}, u32[]{:S(2)}, u32[]{:S(2)}) collective-permute-start(bf16[1,4,1,64,256]{4,3,2,1,0:T(8,128)(2,1)S(1)} %get-tuple-element.67), channel_id=1, source_target_pairs={{0,1},{2,3},{4,5},{6,7},{8,9},{10,11},{12,13},{14,15},{16,17},{18,... | collective-permute-start | bytes 393224 | tf_op jit(solution)/shard_map/ppermute | solution.py:14
  54.2 3.2 collective-permute-start.5
  56.1 3.0 copy-start.1
  319.1 6.9 %copy-start = (f32[3,3,3,256,256]{4,3,2,1,0:T(8,128)S(1)}, f32[3,3,3,256,256]{4,3,2,1,0:T(8,128)}, u32[]{:S(2)}) copy-start(f32[3,3,3,256,256]{4,3,2,1,0:T(8,128)} %get-tuple-element.75) | copy-start | bytes 21233668
Sparse Core Ops, SparseCore 0:
  70.8 248.2 all-reduce.5
where the time goes:
time: 336 us
  waiting for transfers between devices  243 us (72%)
  local copies, waits for them, and re-layouts  25.7 us (8%)
  matrix products  25.7 us (8%)
  starting transfers between devices  21.4 us (6%)
  between operations  15.3 us (5%)
  other arithmetic  4.5 us (1%)
    psum x1, waiting for transfers between devices, shards(): lax.psum((enc_local, dec_local), ('dp', 'tm', 'height'))  241 us
    unnamed x9, local copies, waits for them, and re-layouts  16.3 us
    dot_general x18, matrix products, tap_grads(): lax.dot_general(slab, flat, (((0,), (0,)), ((), ())), preferred_element_t...  15.3 us
    ppermute x3, starting transfers between devices, from_behind(): return lax.ppermute(block, axis, route)  10.8 us
    dot_general x27, matrix products, apply_taps(): jnp.dot(slab, weight[a, b].reshape(3 * chans, outs), preferred_element_ty...  10.4 us
  transfers between devices with their start and end apart: 10, of which 3 were waited for; matrix products, arithmetic and copies ran while one was open for 7% of the time, Pallas kernels for 0%

commit v1 on v0

--- a/solution.py
+++ b/solution.py
@@ -97,7 +97,7 @@
     back = apply_taps(ext_g, flipped)
     dpre = (back * dsilu(pre)).astype(jnp.bfloat16)
     enc_local = tap_grads(ext_x, dpre)
-    enc_grad, dec_grad = lax.psum((enc_local, dec_local), ("dp", "tm", "height"))
+    enc_grad, dec_grad = lax.psum(lax.psum((enc_local, dec_local), ("tm", "height")), "dp")
     return (output, enc_grad, dec_grad)
 
 

time: 336 us -> 643 us (1.91)
  waiting for transfers between devices: 243 us -> 550 us
    psum x1 -> x2, waiting for transfers between devices: 241 us -> 548 us  [the longest x1 286 us: shards(): lax.psum((enc_local, dec_local), ('tm', 'height'))]
  transfers between devices with their start and end apart: 10 -> 11, of which waited for: 3 -> 4; matrix products, arithmetic and copies ran while one was open for 7% -> 4% of each run, Pallas kernels for 0% -> 0%
where the time goes in v1:
time: 643 us
  waiting for transfers between devices  550 us (86%)
  matrix products  25.7 us (4%)
  local copies, waits for them, and re-layouts  25.5 us (4%)
  starting transfers between devices  21.5 us (3%)
  between operations  15.3 us (2%)
    psum x1, waiting for transfers between devices, shards(): lax.psum((enc_local, dec_local), ('tm', 'height'))  286 us
    psum x1, waiting for transfers between devices, shards(): lax.psum(lax.psum((enc_local, dec_local), ('tm', 'height')), 'dp')  262 us
    unnamed x9, local copies, waits for them, and re-layouts  16 us
    dot_general x18, matrix products, tap_grads(): lax.dot_general(slab, flat, (((0,), (0,)), ((), ())), preferred_element_t...  15.3 us
  transfers between devices with their start and end apart: 11, of which 4 were waited for; matrix products, arithmetic and copies ran while one was open for 4% of the time, Pallas kernels for 0%

profile of v1, /device:TPU:0, one launch (start us, length us, event | category | flops | bytes accessed | tf_op | source)
XLA Modules:
  0.0 642.9 jit_solution(18273266485072736124)
XLA Ops:
  7.9 1.1 broadcast_select_fusion
  9.0 4.9 collective-permute-start
  14.0 1.3 collective-permute-start.6
  15.3 6.0 copy.8
  21.3 2.4 reverse_bitcast_fusion
  24.1 1.6 collective-permute-start.7
  25.7 1.3 collective-permute-start.8
  27.4 3.0 collective-permute-start.1
  30.4 1.3 collective-permute-start.2
  31.8 0.5 select_maximum_fusion
  32.3 0.5 fusion.103
  32.8 0.9 collective-permute-done.2
  33.7 0.5 fusion.49
  34.2 0.5 fusion.105
  35.0 0.9 fusion.100
  36.2 0.9 fusion.102
  37.0 0.4 fusion.113
  38.6 0.4 fusion.109
  38.9 0.4 fusion.108
  39.7 0.4 fusion.106
  40.1 0.5 fusion.40
  40.7 4.6 collective-permute-start.3
  45.7 0.4 fusion.128
  46.0 0.4 fusion.127
  46.8 0.4 fusion.125
  47.2 0.4 fusion.124
  47.9 0.4 fusion.122
  48.3 0.6 fusion.41
  48.9 0.4 fusion.18
  49.4 0.4 fusion.17
  49.8 0.4 fusion.16
  50.2 0.4 fusion.15
  50.6 0.4 fusion.14
  51.0 0.4 fusion.13
  51.5 0.4 fusion.12
  51.9 0.4 fusion.11
  52.4 1.8 collective-permute-start.4
  54.2 1.3 collective-permute-start.5
  55.5 0.4 fusion.10
  55.9 1.5 collective-permute-done.5
  57.4 0.5 select_maximum_fusion.3
  57.9 0.5 fusion.104
  58.9 1.3 fusion.9
  60.2 1.3 fusion.8
  61.5 1.3 fusion.7
  62.8 1.3 fusion.6
  64.0 1.3 fusion.5
  65.3 1.3 fusion.4
  66.6 1.3 fusion.3
  67.9 1.3 fusion.2
  69.2 1.3 fusion.1
  70.8 285.6 %all-reduce.8.cloned.1.call-done = (f32[3,3,3,256,256]{4,3,2,1,0:T(8,128)}, f32[3,3,3,256,256]{4,3,2,1,0:T(8,128)}) async-done(((f32[3,3,3,256,256]{4,3,2,1,0:T(8,128)}, f32[3,3,3,256,256]{4,3,2,1,0:T(8,128)}), (f32[3,3,3,256,256]{4,3,2,1,0:T(8,128)}, f32[3,3,3,256,256]{4,3,2,1,0:T(8,128)})) %all-reduce.8.cloned.1.call-update) | async-done | bytes 14155792 | tf_op jit(solution)/shard_map/psum | solution.py:100
  356.4 2.3 fusion.98
  358.7 0.9 fusion.101
  359.6 0.4 fusion.121
  360.0 0.4 fusion.120
  360.3 0.4 fusion.119
  361.1 0.4 fusion.117
  361.5 0.4 fusion.116
  362.6 0.4 fusion.35
  363.1 0.8 add_convert_fusion
  363.8 262.4 %all-reduce.10.cloned.1.call-done = (f32[3,3,3,256,256]{4,3,2,1,0:T(8,128)}, f32[3,3,3,256,256]{4,3,2,1,0:T(8,128)}) async-done(((f32[3,3,3,256,256]{4,3,2,1,0:T(8,128)}, f32[3,3,3,256,256]{4,3,2,1,0:T(8,128)}), (f32[3,3,3,256,256]{4,3,2,1,0:T(8,128)}, f32[3,3,3,256,256]{4,3,2,1,0:T(8,128)})) %all-reduce.10.cloned.1.call-update) | async-done | bytes 14155792 | tf_op jit(solution)/shard_map/psum | solution.py:100
  626.2 6.9 %copy.48 = f32[3,3,3,256,256]{4,3,2,1,0:T(8,128)} copy(f32[3,3,3,256,256]{4,3,2,1,0:T(8,128)} %get-tuple-element.76) | data formatting | bytes 14155776
  633.1 3.0 copy.49
  (37 shorter events, 6.1 us)
Async XLA Ops:
  7.2 349.2 %all-reduce.8.cloned.1.call-start = ((), (), s32[]{:S(2)}) async-start(), calls=%async_computation | async-start | bytes 28311552 | tf_op jit(solution)/shard_map/psum | solution.py:100
  9.0 18.3 %collective-permute-start = (bf16[1,2,4,64,256]{4,3,2,1,0:T(8,128)(2,1)S(1)}, bf16[1,2,4,64,256]{4,3,2,1,0:T(8,128)(2,1)S(1)}, u32[]{:S(2)}, u32[]{:S(2)}) collective-permute-start(bf16[1,2,4,64,256]{4,3,2,1,0:T(8,128)(2,1)S(1)} %get-tuple-element.74), channel_id=1, source_target_pairs={{0,2},{2,4},{4,6},{1,3},{3,5},{5,7},{8,10},{10,12},{12,14},{9,11},... | collective-permute-start | bytes 786440 | tf_op jit(solution)/shard_map/ppermute | solution.py:23
  14.0 10.1 %collective-permute-start.6 = (bf16[1,2,4,64,256]{4,3,2,1,0:T(8,128)(2,1)S(1)}, bf16[1,2,4,64,256]{4,3,2,1,0:T(8,128)(2,1)S(1)}, u32[]{:S(2)}, u32[]{:S(2)}) collective-permute-start(bf16[1,2,4,64,256]{4,3,2,1,0:T(8,128)(2,1)S(1)} %get-tuple-element.73), channel_id=1, source_target_pairs={{2,0},{4,2},{6,4},{3,1},{5,3},{7,5},{10,8},{12,10},{14,12},{11,9},... | collective-permute-start | bytes 786440 | tf_op jit(solution)/shard_map/ppermute | solution.py:23
  23.7 3.3 copy-start.2
  24.1 7.7 %collective-permute-start.7 = (bf16[1,4,1,64,256]{4,3,2,1,0:T(8,128)(2,1)S(1)}, bf16[1,4,1,64,256]{4,3,2,1,0:T(8,128)(2,1)S(1)}, u32[]{:S(2)}, u32[]{:S(2)}) collective-permute-start(bf16[1,4,1,64,256]{4,3,2,1,0:T(8,128)(2,1)S(1)} %get-tuple-element.67), channel_id=1, source_target_pairs={{0,1},{2,3},{4,5},{6,7},{8,9},{10,11},{12,13},{14,15},{16,17},{18,... | collective-permute-start | bytes 393224 | tf_op jit(solution)/shard_map/ppermute | solution.py:14
  25.7 6.1 collective-permute-start.8
  27.4 5.4 collective-permute-start.1
  30.4 3.2 collective-permute-start.2
  40.7 11.6 %collective-permute-start.3 = (bf16[1,2,4,64,256]{4,3,2,1,0:T(8,128)(2,1)S(1)}, bf16[1,2,4,64,256]{4,3,2,1,0:T(8,128)(2,1)S(1)}, u32[]{:S(2)}, u32[]{:S(2)}) collective-permute-start(bf16[1,2,4,64,256]{4,3,2,1,0:T(8,128)(2,1)S(1)} %multiply_convert_fusion), channel_id=1, source_target_pairs={{0,2},{2,4},{4,6},{1,3},{3,5},{5,7},{8,10},{10,12},{12,14},{9,11},... | collective-permute-start | bytes 786440 | tf_op jit(solution)/shard_map/ppermute | solution.py:23
  52.4 3.6 collective-permute-start.4
  54.2 3.2 collective-permute-start.5
  55.9 3.0 copy-start.1
  70.5 555.7 %all-reduce.10.cloned.1.call-start = ((), (), s32[]{:S(2)}) async-start(), calls=%async_computation.1 | async-start | bytes 28311552 | tf_op jit(solution)/shard_map/psum | solution.py:100
  626.2 6.9 %copy-start = (f32[3,3,3,256,256]{4,3,2,1,0:T(8,128)S(1)}, f32[3,3,3,256,256]{4,3,2,1,0:T(8,128)}, u32[]{:S(2)}) copy-start(f32[3,3,3,256,256]{4,3,2,1,0:T(8,128)} %get-tuple-element.77) | copy-start | bytes 21233668
Sparse Core Ops, SparseCore 0:
  70.6 285.6 all-reduce.7
  360.1 266.0 all-reduce.9
